TPU v7x, 32 devices: a whole 2x2x4 slice. The times are simulated.
32 devices in a mesh: aux: 32 (over z, y, x, core).
Axes of the slice: x: 2, y: 2, z: 4, core: 2. Of those that a mesh axis runs over, the one named last changes fastest.
Arguments:
- rho_real: float32 [64, 256, 256], P('aux'), may hold values from -6 to 6
- rho_imag: float32 [64, 256, 256], P('aux'), may hold values from -6 to 6
- hamiltonian: float32 [256, 256], replicated, may hold values from -0.375 to 0.375
- damping: float32 [256], replicated, may hold values from 0.5 to 4
- up_scale: float32 [256], replicated, may hold values from 0.2 to 1
- bath_real: float32 [256], replicated, may hold values from 0.1 to 1
- bath_imag: float32 [256], replicated, may hold values from -1 to -0.1
- link_neighbor: int32 [64, 64], P('aux'), may hold values from 0 to 63, as said below
- link_site: int32 [64, 64], P('aux'), may hold values from 0 to 255, as said below
- link_occupation: int32 [64, 64], P('aux'), may hold values from 0 to 2, as said below
Outputs:
- next_real: float32 [64, 256, 256], P('aux')
- next_imag: float32 [64, 256, 256], P('aux')
Inputs may be any that keep to these rules, and one draw needn't show every extreme that they name: `link_neighbor`: matrix m is held by device m // 2. Of the links of one device's matrices, at most 8 name matrices held by any one device, and in every draw exactly 8 do for some pair of devices. `link_site`: the 64 sites of one matrix are distinct. `link_occupation`: links to higher tiers have occupation 1. The last 3 links of a matrix hold its own occupations, which sum to 1 or 2; a zero marks an unoccupied site.
All inputs are finite; a program needn't handle non-finite values.
Results may differ from a plain program's by a relative error of at most 0.0001.
Values sent between devices are 32-bit elements; how exact they have to be, the bound alone decides.
A program may use at most 64 MiB of HBM per device.

v0:
```python
import functools

import jax
import jax.numpy as jnp
from jax import lax
from jax.experimental import pallas as pl
from jax.experimental.pallas import tpu as pltpu
from jax.sharding import PartitionSpec as P

DOWN = 3
STEP_SIZE = 0.25
MESH = pl.DeviceIdType.MESH
F32 = jnp.float32
BF16 = jnp.bfloat16
NN = (((1,), (0,)), ((), ()))
NT = (((1,), (1,)), ((), ()))


def split(value):
    high = value.astype(BF16)
    return high, (value - high.astype(F32)).astype(BF16)


def dot(a, b, dims=NN):
    return lax.dot_general(a, b, dims, preferred_element_type=F32)


def exact_dot(a, b):
    return jnp.dot(a, b, precision=lax.Precision.HIGHEST, preferred_element_type=F32)


def kernel(
    peers,
    cap,
    mat_dev,
    link_count,
    sites,
    rho_re,
    rho_im,
    ham_in,
    damping,
    up_scale,
    bath_re,
    bath_im,
    table,
    cur_re,
    cur_im,
    send,
    recv,
    req_send,
    req_recv,
    ham,
    acc,
    base,
    pick,
    put,
    coef_re,
    coef_im,
    stack,
    wide,
    terms,
    req_sems,
    send_sems,
    recv_sems,
):
    me = lax.axis_index("aux")
    slots = peers * cap
    links = mat_dev * link_count

    barrier = pltpu.get_barrier_semaphore()

    def greet(k, carry):
        pl.semaphore_signal(
            barrier, inc=1, device_id=(lax.rem(me + k, peers),), device_id_type=MESH
        )
        return carry

    lax.fori_loop(1, peers, greet, 0)

    neighbor = table[0:1, :]
    site = table[1:2, :]
    occupied = table[2:3, :]
    owner = neighbor // mat_dev
    owner_here = jnp.broadcast_to(owner.astype(F32), (links, links))
    owner_there = owner_here.T
    first = lax.broadcasted_iota(jnp.int32, (links, links), 0)
    second = lax.broadcasted_iota(jnp.int32, (links, links), 1)
    earlier = jnp.where((owner_here == owner_there) & (first < second), 1.0, 0.0)
    rank = jnp.sum(earlier, axis=0, keepdims=True).astype(jnp.int32)
    slot = owner * cap + rank
    lane = lax.broadcasted_iota(jnp.int32, (1, links), 1)
    holder = lane // link_count
    upward = (lane - holder * link_count < link_count - DOWN).astype(jnp.int32)
    code = site + sites * (
        (neighbor - owner * mat_dev) + mat_dev * (holder + mat_dev * (upward + 2 * occupied))
    )
    slot_index = lax.broadcasted_iota(jnp.int32, (slots, links), 0)
    code_slot = (
        jnp.sum(
            jnp.where(slot_index == slot, (code + 1).astype(F32), 0.0), axis=1, keepdims=True
        ).astype(jnp.int32)
        - 1
    )
    used = code_slot >= 0
    safe = jnp.maximum(code_slot, 0)
    wanted = jnp.where(used, safe % (sites * mat_dev), -1)
    req_send[...] = jnp.broadcast_to(wanted, (slots, 128)).reshape(peers, cap, 128)

    pl.semaphore_wait(barrier, peers - 1)

    def request(k, carry):
        peer = lax.rem(me + k, peers)
        pltpu.make_async_remote_copy(
            src_ref=req_send.at[peer],
            dst_ref=req_recv.at[me],
            send_sem=req_sems.at[0],
            recv_sem=req_sems.at[1],
            device_id=(peer,),
            device_id_type=MESH,
        ).start()
        return carry

    lax.fori_loop(1, peers, request, 0)
    req_recv[me] = req_send[me]

    site_slot = jnp.where(used, safe % sites, -1)
    rest = safe // (sites * mat_dev)
    holder_slot = jnp.where(used, rest % mat_dev, -1)
    rest = rest // mat_dev
    up_slot = used & (rest % 2 == 1)
    occ_slot = jnp.where(used, (rest // 2).astype(F32), 0.0)
    own_site = lax.broadcasted_iota(jnp.int32, (slots, sites), 1) == site_slot

    def look_up(ref):
        return jnp.sum(jnp.where(own_site, ref[...], 0.0), axis=1, keepdims=True)

    part_re = jnp.where(up_slot, 0.0, occ_slot * look_up(bath_im))
    part_im = jnp.where(up_slot, look_up(up_scale) * jnp.sqrt(occ_slot), occ_slot * look_up(bath_re))
    coef_re[...] = jnp.broadcast_to(part_re, (slots, sites))
    coef_im[...] = jnp.broadcast_to(part_im, (slots, sites))
    rate = jnp.where(up_slot, 0.0, occ_slot * look_up(damping))
    gamma = [
        jnp.sum(jnp.where(holder_slot == m, rate, 0.0), axis=0, keepdims=True)
        for m in range(mat_dev)
    ]
    target = jnp.where(used, holder_slot * sites + site_slot, -1).astype(F32)
    target = jnp.broadcast_to(target, (slots, 128)).T[0:1, :].astype(jnp.int32)
    placed = lax.broadcasted_iota(jnp.int32, (mat_dev * sites, slots), 0) == target
    placed = jnp.where(placed, 1.0, 0.0).astype(BF16)
    put[:, 0:slots] = placed
    put[:, slots:] = placed

    ham[...] = 0.5 * (ham_in[...] + ham_in[...].T)
    cur_re[...] = rho_re[...]
    cur_im[...] = rho_im[...]
    acc[...] = jnp.zeros_like(acc)

    pltpu.make_async_copy(
        req_recv.at[pl.ds(0, peers - 1)], req_recv.at[pl.ds(0, peers - 1)], req_sems.at[1]
    ).wait()
    asked = req_recv[...].reshape(slots, 128)[:, 0:1]
    depth = mat_dev * sites
    picked = lax.broadcasted_iota(jnp.int32, (slots, depth), 1) == asked
    picked = jnp.where(picked, 1.0, 0.0).astype(BF16)
    pick[:, 0:depth] = picked
    pick[:, depth:] = picked

    def stage(t, carry):
        for c, cur in enumerate((cur_re, cur_im)):
            for m in range(mat_dev):
                high, low = split(cur[m])
                stack[c, m * sites : (m + 1) * sites, :] = high
                stack[c, depth + m * sites : depth + (m + 1) * sites, :] = low
                wide[c, :, m * sites : (m + 1) * sites] = high
                wide[c, :, depth + m * sites : depth + (m + 1) * sites] = low
        for c in range(2):
            send[t, :, c] = dot(pick[...], stack[c]).reshape(peers, cap, sites)
            send[t, :, 2 + c] = dot(pick[...], wide[c], NT).reshape(peers, cap, sites)

        def post(k, carry):
            peer = lax.rem(me + k, peers)
            pltpu.make_async_remote_copy(
                src_ref=send.at[t, peer],
                dst_ref=recv.at[t, me],
                send_sem=send_sems.at[t],
                recv_sem=recv_sems.at[t],
                device_id=(peer,),
                device_id_type=MESH,
            ).start()
            return carry

        lax.fori_loop(peers // 2, peers, post, 0)
        lax.fori_loop(1, peers // 2, post, 0)
        recv[t, me] = send[t, me]

        last = t == 3
        weight = jnp.where(last, STEP_SIZE / 6.0, jnp.where(t == 2, STEP_SIZE, 0.5 * STEP_SIZE))
        share = jnp.where(t == 0, -1.0 / 3.0, jnp.where(t == 2, 2.0 / 3.0, 1.0 / 3.0))
        keep = jnp.where(last, 0.0, 1.0)
        for m in range(mat_dev):
            here_re, here_im = cur_re[m], cur_im[m]
            acc_re = acc[m, 0] + share * here_re
            acc_im = acc[m, 1] + share * here_im
            acc[m, 0] = acc_re
            acc[m, 1] = acc_im
            comm_re = exact_dot(ham[...], here_re) - exact_dot(here_re, ham[...])
            comm_im = exact_dot(ham[...], here_im) - exact_dot(here_im, ham[...])
            from_re = jnp.where(last, acc_re, rho_re[m])
            from_im = jnp.where(last, acc_im, rho_im[m])
            base[m, 0] = from_re + weight * (comm_im - gamma[m] * here_re)
            base[m, 1] = from_im - weight * (comm_re + gamma[m] * here_im)

        pltpu.make_async_copy(
            recv.at[t, pl.ds(0, peers - 1)], recv.at[t, pl.ds(0, peers - 1)], recv_sems.at[t]
        ).wait()
        pieces = [recv[t, :, q].reshape(slots, sites) for q in range(4)]
        by_re = weight * coef_re[...]
        by_im = weight * coef_im[...]
        added = []
        for q, term in enumerate(
            (
                by_re * pieces[0] + by_im * pieces[1],
                by_re * pieces[1] - by_im * pieces[0],
                by_re * pieces[2] - by_im * pieces[3],
                by_re * pieces[3] + by_im * pieces[2],
            )
        ):
            high, low = split(term)
            terms[q, 0:slots, :] = high
            terms[q, slots:, :] = low
            added.append(dot(put[...], terms[q]))
        for c, cur in enumerate((cur_re, cur_im)):
            for m in range(mat_dev):
                rows = slice(m * sites, (m + 1) * sites)
                cur[m] = base[m, c] + added[c][rows] + added[2 + c][rows].T
        return carry

    lax.fori_loop(0, 4, stage, 0)

    pltpu.make_async_copy(
        req_send.at[pl.ds(0, peers - 1)], req_send.at[pl.ds(0, peers - 1)], req_sems.at[0]
    ).wait()
    for t in range(4):
        pltpu.make_async_copy(
            send.at[t, pl.ds(0, peers - 1)], send.at[t, pl.ds(0, peers - 1)], send_sems.at[t]
        ).wait()


def local(
    rho_real,
    rho_imag,
    hamiltonian,
    damping,
    up_scale,
    bath_real,
    bath_imag,
    link_neighbor,
    link_site,
    link_occupation,
):
    peers = lax.axis_size("aux")
    mat_dev, link_count = link_neighbor.shape
    sites = rho_real.shape[1]
    links = mat_dev * link_count
    cap = -(-max(2, 2 * links // peers) // 8) * 8
    slots = peers * cap
    table = jnp.stack([link_neighbor, link_site, link_occupation]).reshape(3, links)
    vmem = pl.BlockSpec(memory_space=pltpu.VMEM)
    state = jax.ShapeDtypeStruct(rho_real.shape, F32)
    return pl.pallas_call(
        functools.partial(kernel, peers, cap, mat_dev, link_count, sites),
        out_shape=(state, state),
        in_specs=[vmem] * 8,
        out_specs=(vmem, vmem),
        scratch_shapes=[
            pltpu.VMEM((4, peers, 4, cap, sites), F32),
            pltpu.VMEM((4, peers, 4, cap, sites), F32),
            pltpu.VMEM((peers, cap, 128), jnp.int32),
            pltpu.VMEM((peers, cap, 128), jnp.int32),
            pltpu.VMEM((sites, sites), F32),
            pltpu.VMEM((mat_dev, 2, sites, sites), F32),
            pltpu.VMEM((mat_dev, 2, sites, sites), F32),
            pltpu.VMEM((slots, 2 * mat_dev * sites), BF16),
            pltpu.VMEM((mat_dev * sites, 2 * slots), BF16),
            pltpu.VMEM((slots, sites), F32),
            pltpu.VMEM((slots, sites), F32),
            pltpu.VMEM((2, 2 * mat_dev * sites, sites), BF16),
            pltpu.VMEM((2, sites, 2 * mat_dev * sites), BF16),
            pltpu.VMEM((4, 2 * slots, sites), BF16),
            pltpu.SemaphoreType.DMA((2,)),
            pltpu.SemaphoreType.DMA((4,)),
            pltpu.SemaphoreType.DMA((4,)),
        ],
        compiler_params=pltpu.CompilerParams(
            collective_id=0, has_side_effects=True, vmem_limit_bytes=60 * 1024 * 1024
        ),
    )(
        rho_real,
        rho_imag,
        hamiltonian,
        damping.reshape(1, sites),
        up_scale.reshape(1, sites),
        bath_real.reshape(1, sites),
        bath_imag.reshape(1, sites),
        table,
    )


def solution(mesh):
    split_3 = P("aux", None, None)
    split_2 = P("aux", None)
    in_specs = (split_3, split_3, P(), P(), P(), P(), P(), split_2, split_2, split_2)
    return jax.shard_map(
        local, mesh=mesh, in_specs=in_specs, out_specs=(split_3, split_3), check_vma=False
    )
```

profile of v0, /device:TPU:0, one launch (start us, length us, event | category | flops | bytes accessed | tf_op | source)
XLA Modules:
  0.0 119.7 jit_solution(8868442738021636529)
XLA Ops:
  0.6 0.0 copy-start.1
  0.6 0.7 copy-done.1
  1.3 0.0 copy-start.2
  1.3 0.1 stack.12
  1.4 0.6 copy-done.2
  2.0 0.0 copy-start.3
  2.0 0.1 stack.13
  2.1 0.6 copy-done.3
  2.7 0.1 stack.14
  2.8 0.6 pad_add_fusion.table
  3.3 113.7 %shard_map.113 = (f32[2,256,256]{2,1,0:T(8,128)}, f32[2,256,256]{2,1,0:T(8,128)}) custom-call(f32[2,256,256]{2,1,0:T(8,128)} %rho_re.1, f32[2,256,256]{2,1,0:T(8,128)} %rho_im.1, f32[256,256]{1,0:T(8,128)} %ham_in.1, f32[1,256]{1,0:T(1,128)} %bitcast.4, f32[1,256]{1,0:T(1,128)} %bitcast.5, f32[1,256]{1,0:T(1,128)} %bitcast.6, f32[1,256]{1,0:T(1,128)} %bitcast.7, ...), custom_call_target="tpu_custom_call" | custom-call | tf_op jit(solution)/shard_map/pallas_call | solution.py:270
  117.0 0.0 copy-start
  117.0 1.9 %copy.14 = f32[2,256,256]{2,1,0:T(8,128)} copy(f32[2,256,256]{2,1,0:T(8,128)} %get-tuple-element.4) | data formatting | bytes 1048576
  118.9 0.0 copy-done
  119.0 0.8 copy.15
Async XLA Ops:
  0.6 0.7 copy-start.1
  1.3 0.7 copy-start.2
  2.0 0.7 copy-start.3
  117.0 1.9 %copy-start = (f32[2,256,256]{2,1,0:T(8,128)S(1)}, f32[2,256,256]{2,1,0:T(8,128)}, u32[]{:S(2)}) copy-start(f32[2,256,256]{2,1,0:T(8,128)} %get-tuple-element.5) | copy-start | bytes 1572868
where the time goes:
time: 120 us
  Pallas kernels  114 us (95%)
  local copies, waits for them, and re-layouts  4.83 us (4%)
    pallas_call x1, Pallas kernels, local(): pl.pallas_call(functools.partial(kernel, peers, cap, mat_dev, link_count,...  114 us
    unnamed x10, local copies, waits for them, and re-layouts  4.59 us

commit v1 on v0

--- a/solution.py
+++ b/solution.py
@@ -246,27 +246,10 @@
         ).wait()
 
 
-def local(
-    rho_real,
-    rho_imag,
-    hamiltonian,
-    damping,
-    up_scale,
-    bath_real,
-    bath_imag,
-    link_neighbor,
-    link_site,
-    link_occupation,
-):
-    peers = lax.axis_size("aux")
-    mat_dev, link_count = link_neighbor.shape
-    sites = rho_real.shape[1]
-    links = mat_dev * link_count
-    cap = -(-max(2, 2 * links // peers) // 8) * 8
+def run_plain(peers, cap, mat_dev, link_count, sites, arrays):
     slots = peers * cap
-    table = jnp.stack([link_neighbor, link_site, link_occupation]).reshape(3, links)
     vmem = pl.BlockSpec(memory_space=pltpu.VMEM)
-    state = jax.ShapeDtypeStruct(rho_real.shape, F32)
+    state = jax.ShapeDtypeStruct((mat_dev, sites, sites), F32)
     return pl.pallas_call(
         functools.partial(kernel, peers, cap, mat_dev, link_count, sites),
         out_shape=(state, state),
@@ -294,7 +277,440 @@
         compiler_params=pltpu.CompilerParams(
             collective_id=0, has_side_effects=True, vmem_limit_bytes=60 * 1024 * 1024
         ),
-    )(
+    )(*arrays)
+
+
+DIRECT = 4
+PACKED = 24
+
+
+def read_tables(peers, mat_dev, table, all_tables, worst, slab, landed, send_sem, recv_sem):
+    me = lax.axis_index("aux")
+    links = table.shape[1]
+    barrier = pltpu.get_barrier_semaphore()
+
+    def greet(k, carry):
+        pl.semaphore_signal(
+            barrier, inc=1, device_id=(lax.rem(me + k, peers),), device_id_type=MESH
+        )
+        return carry
+
+    lax.fori_loop(1, peers, greet, 0)
+    slab[...] = jnp.zeros_like(slab)
+    slab[0:3, :] = table[...]
+    pl.semaphore_wait(barrier, peers - 1)
+
+    def post(k, carry):
+        peer = lax.rem(me + k, peers)
+        pltpu.make_async_remote_copy(
+            src_ref=slab,
+            dst_ref=landed.at[me],
+            send_sem=send_sem,
+            recv_sem=recv_sem,
+            device_id=(peer,),
+            device_id_type=MESH,
+        ).start()
+        return carry
+
+    lax.fori_loop(1, peers, post, 0)
+    landed[me] = slab[...]
+    others = landed.at[pl.ds(0, peers - 1)]
+    pltpu.make_async_copy(others, others, recv_sem).wait()
+    tables = landed[...]
+    neighbor = tables[:, 0, :]
+    all_tables[0] = neighbor
+    all_tables[1] = tables[:, 1, :]
+    owner = neighbor // mat_dev
+    lane = lax.broadcasted_iota(jnp.int32, (peers, links), 1)
+    row = lax.broadcasted_iota(jnp.int32, (peers, links), 0)
+    counts = jnp.zeros((peers, links), F32)
+    for d in range(peers):
+        count = jnp.sum(jnp.where(owner == d, 1.0, 0.0), axis=1, keepdims=True)
+        counts = jnp.where(lane == d, count, counts)
+    half = peers // 2
+    apart = (lane // half) != (row // half)
+    over = jnp.where(apart & (lane < peers), jnp.maximum(counts - DIRECT, 0.0), 0.0)
+    most = jnp.max(jnp.sum(over, axis=0, keepdims=True), axis=1, keepdims=True)
+    worst[...] = jnp.broadcast_to(most, worst.shape).astype(jnp.int32)
+    pltpu.make_async_copy(others, others, send_sem).wait()
+
+
+def packed_kernel(
+    peers,
+    mat_dev,
+    link_count,
+    sites,
+    rho_re,
+    rho_im,
+    ham_in,
+    damping,
+    up_scale,
+    bath_re,
+    bath_im,
+    table,
+    all_tables,
+    cur_re,
+    cur_im,
+    send_low,
+    send_high,
+    send_pack,
+    send_relay,
+    recv_low,
+    recv_high,
+    recv_pack,
+    ham,
+    acc,
+    base,
+    ask_high,
+    spread_all,
+    pick,
+    spread,
+    put,
+    coef_re,
+    coef_im,
+    stack,
+    wide,
+    terms,
+    send_sems,
+    recv_sems,
+):
+    me = lax.axis_index("aux")
+    half = peers // 2
+    links = mat_dev * link_count
+    depth = mat_dev * sites
+    block = peers * 8
+    slots = 2 * block
+    mirror = lax.rem(me + half, peers)
+    home = (me // half) * half
+    place = me - home
+    away = half - home
+
+    barrier = pltpu.get_barrier_semaphore()
+
+    def greet(k, carry):
+        pl.semaphore_signal(
+            barrier, inc=1, device_id=(lax.rem(me + k, peers),), device_id_type=MESH
+        )
+        return carry
+
+    lax.fori_loop(1, peers, greet, 0)
+
+    neighbors = all_tables[0]
+    wanted_all = ((neighbors % mat_dev) * sites + all_tables[1] + 1).astype(F32)
+    first = lax.broadcasted_iota(jnp.int32, (links, links), 0)
+    second = lax.broadcasted_iota(jnp.int32, (links, links), 1)
+    before = jnp.where(first < second, 1.0, 0.0)
+    lane_of = lax.broadcasted_iota(jnp.int32, (peers, links), 1)
+    row_of = lax.broadcasted_iota(jnp.int32, (peers, links), 0)
+
+    def asked_of(owner):
+        mask = neighbors // mat_dev == owner
+        ranks = dot(jnp.where(mask, 1.0, 0.0).astype(BF16), before.astype(BF16))
+        out = jnp.zeros((peers, links), F32)
+        for k in range(2 * DIRECT):
+            found = jnp.sum(
+                jnp.where(mask & (ranks == k), wanted_all, 0.0), axis=1, keepdims=True
+            )
+            out = jnp.where(lane_of == k, found, out)
+        return out
+
+    def as_rows(value, start):
+        lane = lax.broadcasted_iota(jnp.int32, (peers, 8, links), 2)
+        row = lax.broadcasted_iota(jnp.int32, (peers, 8, links), 1)
+        spot = jnp.where(lane == start + row % DIRECT, value.reshape(peers, 1, links), 0.0)
+        return jnp.sum(spot, axis=2, keepdims=True).reshape(block, 1)
+
+    part = (lax.broadcasted_iota(jnp.int32, (block, 1), 0) // DIRECT) % 2
+
+    def ask_matrix(rows):
+        target = jnp.where(rows > 0.5, rows.astype(jnp.int32) - 1 + depth * part, -1)
+        match = lax.broadcasted_iota(jnp.int32, (block, 2 * depth), 1) == target
+        return jnp.where(match, 1.0, 0.0).astype(BF16)
+
+    earlier_row = lax.broadcasted_iota(jnp.int32, (peers, peers), 0)
+    earlier_col = lax.broadcasted_iota(jnp.int32, (peers, peers), 1)
+    above = jnp.where(earlier_col < earlier_row, 1.0, 0.0).astype(BF16)
+
+    def packing(asked, group):
+        keep = (row_of // half == group) & (lane_of >= DIRECT) & (asked > 0.5)
+        flags = jnp.where(keep, 1.0, 0.0)
+        rows_before = jnp.sum(dot(above, flags.astype(BF16)), axis=1, keepdims=True)
+        position = rows_before + dot(flags.astype(BF16), before.astype(BF16))
+        rows = as_rows(jnp.where(keep, position + 1.0, 0.0), DIRECT).astype(jnp.int32)
+        target = jnp.where((rows > 0) & (rows <= PACKED), rows - 1 + PACKED * part, -1)
+        return lax.broadcasted_iota(jnp.int32, (block, 128), 1) == target
+
+    mine = asked_of(me)
+    asked_mirror = asked_of(mirror)
+    high_all = ask_matrix(as_rows(mine, DIRECT))
+    ask_high[...] = high_all.astype(F32)
+    pack = jnp.where(packing(mine, 1 - me // half), 1.0, 0.0).T[0 : 2 * PACKED, :].astype(BF16)
+    spread_all[...] = jnp.where(packing(asked_mirror, me // half), 1.0, 0.0)
+    pick[0:block, 0 : 2 * depth] = ask_matrix(as_rows(mine, 0))
+    pick[block : block + half * 8, 0 : 2 * depth] = ask_high[
+        pl.ds(pl.multiple_of(home * 8, 128), half * 8), :
+    ].astype(BF16)
+    pick[block + half * 8 :, 0 : 2 * depth] = dot(pack, high_all).astype(BF16)
+    pick[:, 2 * depth :] = pick[:, 0 : 2 * depth]
+    spread[...] = spread_all[pl.ds(pl.multiple_of(home * 8, 128), half * 8), :].astype(BF16)
+
+    neighbor = table[0:1, :]
+    owner = neighbor // mat_dev
+    owner_here = jnp.broadcast_to(owner.astype(F32), (links, links))
+    same = jnp.where((owner_here == owner_here.T) & (first < second), 1.0, 0.0)
+    rank = jnp.sum(same, axis=0, keepdims=True).astype(jnp.int32)
+    landing = (rank // DIRECT) * block + owner * 8 + rank % DIRECT
+    lane = lax.broadcasted_iota(jnp.int32, (1, links), 1)
+    holder = lane // link_count
+    upward = (lane - holder * link_count < link_count - DOWN).astype(jnp.int32)
+    code = table[1:2, :] + sites * (holder + mat_dev * (upward + 2 * table[2:3, :]))
+    slot_index = lax.broadcasted_iota(jnp.int32, (slots, links), 0)
+    slot_base = slot_index - DIRECT * ((slot_index // DIRECT) % 2)
+    code_slot = (
+        jnp.sum(
+            jnp.where(slot_base == landing, (code + 1).astype(F32), 0.0), axis=1, keepdims=True
+        ).astype(jnp.int32)
+        - 1
+    )
+    used = code_slot >= 0
+    safe = jnp.maximum(code_slot, 0)
+    site_slot = jnp.where(used, safe % sites, -1)
+    rest = safe // sites
+    holder_slot = jnp.where(used, rest % mat_dev, -1)
+    rest = rest // mat_dev
+    up_slot = used & (rest % 2 == 1)
+    occ_slot = jnp.where(used, (rest // 2).astype(F32), 0.0)
+    own_site = lax.broadcasted_iota(jnp.int32, (slots, sites), 1) == site_slot
+
+    def look_up(ref):
+        return jnp.sum(jnp.where(own_site, ref[...], 0.0), axis=1, keepdims=True)
+
+    component = (lax.broadcasted_iota(jnp.int32, (slots, 1), 0) // DIRECT) % 2
+    part_re = jnp.where(up_slot, 0.0, occ_slot * look_up(bath_im))
+    part_im = jnp.where(up_slot, look_up(up_scale) * jnp.sqrt(occ_slot), occ_slot * look_up(bath_re))
+    part_im = jnp.where(component == 0, part_im, -part_im)
+    coef_re[...] = jnp.broadcast_to(part_re, (slots, sites))
+    coef_im[...] = jnp.broadcast_to(part_im, (slots, sites))
+    rate = jnp.where(up_slot | (component == 1), 0.0, occ_slot * look_up(damping))
+    gamma = [
+        jnp.sum(jnp.where(holder_slot == m, rate, 0.0), axis=0, keepdims=True)
+        for m in range(mat_dev)
+    ]
+    target = jnp.where(used, component * depth + holder_slot * sites + site_slot, -1)
+    target = jnp.broadcast_to(target.astype(F32), (slots, 128)).T[0:1, :].astype(jnp.int32)
+    placed = lax.broadcasted_iota(jnp.int32, (2 * depth, slots), 0) == target
+    placed = jnp.where(placed, 1.0, 0.0).astype(BF16)
+    put[:, 0:slots] = placed
+    put[:, slots:] = placed
+
+    ham[...] = 0.5 * (ham_in[...] + ham_in[...].T)
+    cur_re[...] = rho_re[...]
+    cur_im[...] = rho_im[...]
+    acc[...] = jnp.zeros_like(acc)
+    pl.semaphore_wait(barrier, peers - 1)
+
+    def send(source, target, t, kind, peer):
+        return pltpu.make_async_remote_copy(
+            src_ref=source,
+            dst_ref=target,
+            send_sem=send_sems.at[t, kind],
+            recv_sem=recv_sems.at[t, kind % 3],
+            device_id=(peer,),
+            device_id_type=MESH,
+        )
+
+    def stage(t, carry):
+        for c, cur in enumerate((cur_re, cur_im)):
+            for m in range(mat_dev):
+                high, low = split(cur[m])
+                at = c * depth + m * sites
+                stack[at : at + sites, :] = high
+                stack[2 * depth + at : 2 * depth + at + sites, :] = low
+                wide[:, at : at + sites] = high
+                wide[:, 2 * depth + at : 2 * depth + at + sites] = low
+        for p, pieces in enumerate((dot(pick[...], stack[...]), dot(pick[...], wide[...], NT))):
+            send_low[t, :, p] = pieces[0:block].reshape(peers, 8, sites)
+            send_high[t, :, p] = pieces[block : block + half * 8].reshape(half, 8, sites)
+            send_pack[t, p] = pieces[block + half * 8 :]
+
+        send(send_pack.at[t], recv_pack.at[t], t, 2, mirror).start()
+
+        def across(k, c):
+            peer = away + lax.rem(place + k, half)
+            send(send_low.at[t, peer], recv_low.at[t, me], t, 0, peer).start()
+            return c
+
+        def near(k, c):
+            there = lax.rem(place + k, half)
+            peer = home + there
+            send(send_low.at[t, peer], recv_low.at[t, me], t, 0, peer).start()
+            send(send_high.at[t, there], recv_high.at[t, me], t, 1, peer).start()
+            return c
+
+        lax.fori_loop(0, half, across, 0)
+        lax.fori_loop(1, half, near, 0)
+        recv_low[t, me] = send_low[t, me]
+        recv_high[t, me] = send_high[t, place]
+
+        last = t == 3
+        weight = jnp.where(last, STEP_SIZE / 6.0, jnp.where(t == 2, STEP_SIZE, 0.5 * STEP_SIZE))
+        share = jnp.where(t == 0, -1.0 / 3.0, jnp.where(t == 2, 2.0 / 3.0, 1.0 / 3.0))
+
+        def alone(m):
+            here_re, here_im = cur_re[m], cur_im[m]
+            acc_re = acc[m, 0] + share * here_re
+            acc_im = acc[m, 1] + share * here_im
+            acc[m, 0] = acc_re
+            acc[m, 1] = acc_im
+            comm_re = exact_dot(ham[...], here_re) - exact_dot(here_re, ham[...])
+            comm_im = exact_dot(ham[...], here_im) - exact_dot(here_im, ham[...])
+            from_re = jnp.where(last, acc_re, rho_re[m])
+            from_im = jnp.where(last, acc_im, rho_im[m])
+            base[m, 0] = from_re + weight * (comm_im - gamma[m] * here_re)
+            base[m, 1] = from_im - weight * (comm_re + gamma[m] * here_im)
+
+        for m in range(mat_dev // 2):
+            alone(m)
+
+        send(send_pack.at[t], recv_pack.at[t], t, 2, mirror).wait_recv()
+        for p in range(2):
+            high, low = split(recv_pack[t, p])
+            relay = dot(spread[:, 0 : 2 * PACKED], high) + dot(spread[:, 0 : 2 * PACKED], low)
+            send_relay[t, :, p] = relay.reshape(half, 8, sites)
+
+        def pass_on(k, c):
+            there = lax.rem(place + k, half)
+            send(
+                send_relay.at[t, there], recv_high.at[t, mirror], t, 4, home + there
+            ).start()
+            return c
+
+        lax.fori_loop(1, half, pass_on, 0)
+        recv_high[t, mirror] = send_relay[t, place]
+
+        for m in range(mat_dev // 2, mat_dev):
+            alone(m)
+
+        lows = recv_low.at[t, pl.ds(0, peers - 1)]
+        pltpu.make_async_copy(lows, lows, recv_sems.at[t, 0]).wait()
+        highs = recv_high.at[t, pl.ds(0, peers - 2)]
+        pltpu.make_async_copy(highs, highs, recv_sems.at[t, 1]).wait()
+        by_re = weight * coef_re[...]
+        by_im = weight * coef_im[...]
+        added = []
+        for p in range(2):
+            whole = jnp.concatenate([recv_low[t, :, p], recv_high[t, :, p]], axis=0)
+            turned = pltpu.roll(whole, DIRECT, 1).reshape(slots, sites)
+            whole = whole.reshape(slots, sites)
+            cross = by_im * turned
+            term = by_re * whole + (cross if p == 0 else -cross)
+            high, low = split(term)
+            terms[p, 0:slots, :] = high
+            terms[p, slots:, :] = low
+            added.append(dot(put[...], terms[p]))
+        for c, cur in enumerate((cur_re, cur_im)):
+            for m in range(mat_dev):
+                rows = slice(c * depth + m * sites, c * depth + (m + 1) * sites)
+                cur[m] = base[m, c] + added[0][rows] + added[1][rows].T
+        return carry
+
+    lax.fori_loop(0, 4, stage, 0)
+
+    def drain(t, carry):
+        lows = send_low.at[t, pl.ds(0, peers - 1)]
+        pltpu.make_async_copy(lows, lows, send_sems.at[t, 0]).wait()
+        highs = send_high.at[t, pl.ds(0, half - 1)]
+        pltpu.make_async_copy(highs, highs, send_sems.at[t, 1]).wait()
+        send(send_pack.at[t], recv_pack.at[t], t, 2, mirror).wait_send()
+        relays = send_relay.at[t, pl.ds(0, half - 1)]
+        pltpu.make_async_copy(relays, relays, send_sems.at[t, 4]).wait()
+        return carry
+
+    lax.fori_loop(0, 4, drain, 0)
+
+
+def run_packed(peers, mat_dev, link_count, sites, arrays):
+    half = peers // 2
+    depth = mat_dev * sites
+    slots = peers * 16
+    rows = peers * 8 + half * 8 + 2 * PACKED
+    vmem = pl.BlockSpec(memory_space=pltpu.VMEM)
+    state = jax.ShapeDtypeStruct((mat_dev, sites, sites), F32)
+    return pl.pallas_call(
+        functools.partial(packed_kernel, peers, mat_dev, link_count, sites),
+        out_shape=(state, state),
+        in_specs=[vmem] * 9,
+        out_specs=(vmem, vmem),
+        scratch_shapes=[
+            pltpu.VMEM((4, peers, 2, 8, sites), F32),
+            pltpu.VMEM((4, half, 2, 8, sites), F32),
+            pltpu.VMEM((4, 2, 2 * PACKED, sites), F32),
+            pltpu.VMEM((4, half, 2, 8, sites), F32),
+            pltpu.VMEM((4, peers, 2, 8, sites), F32),
+            pltpu.VMEM((4, peers, 2, 8, sites), F32),
+            pltpu.VMEM((4, 2, 2 * PACKED, sites), F32),
+            pltpu.VMEM((sites, sites), F32),
+            pltpu.VMEM((mat_dev, 2, sites, sites), F32),
+            pltpu.VMEM((mat_dev, 2, sites, sites), F32),
+            pltpu.VMEM((peers * 8, 2 * depth), F32),
+            pltpu.VMEM((peers * 8, 128), F32),
+            pltpu.VMEM((rows, 4 * depth), BF16),
+            pltpu.VMEM((half * 8, 128), BF16),
+            pltpu.VMEM((2 * depth, 2 * slots), BF16),
+            pltpu.VMEM((slots, sites), F32),
+            pltpu.VMEM((slots, sites), F32),
+            pltpu.VMEM((4 * depth, sites), BF16),
+            pltpu.VMEM((sites, 4 * depth), BF16),
+            pltpu.VMEM((2, 2 * slots, sites), BF16),
+            pltpu.SemaphoreType.DMA((4, 5)),
+            pltpu.SemaphoreType.DMA((4, 3)),
+        ],
+        compiler_params=pltpu.CompilerParams(
+            collective_id=1, has_side_effects=True, vmem_limit_bytes=60 * 1024 * 1024
+        ),
+    )(*arrays)
+
+
+def run_tables(peers, mat_dev, table):
+    vmem = pl.BlockSpec(memory_space=pltpu.VMEM)
+    links = table.shape[1]
+    return pl.pallas_call(
+        functools.partial(read_tables, peers, mat_dev),
+        out_shape=(
+            jax.ShapeDtypeStruct((2, peers, links), jnp.int32),
+            jax.ShapeDtypeStruct((8, 128), jnp.int32),
+        ),
+        in_specs=[vmem],
+        out_specs=(vmem, vmem),
+        scratch_shapes=[
+            pltpu.VMEM((8, links), jnp.int32),
+            pltpu.VMEM((peers, 8, links), jnp.int32),
+            pltpu.SemaphoreType.DMA,
+            pltpu.SemaphoreType.DMA,
+        ],
+        compiler_params=pltpu.CompilerParams(collective_id=2, has_side_effects=True),
+    )(table)
+
+
+def local(
+    rho_real,
+    rho_imag,
+    hamiltonian,
+    damping,
+    up_scale,
+    bath_real,
+    bath_imag,
+    link_neighbor,
+    link_site,
+    link_occupation,
+):
+    peers = lax.axis_size("aux")
+    mat_dev, link_count = link_neighbor.shape
+    sites = rho_real.shape[1]
+    links = mat_dev * link_count
+    cap = -(-max(2, 2 * links // peers) // 8) * 8
+    table = jnp.stack([link_neighbor, link_site, link_occupation]).reshape(3, links)
+    arrays = (
         rho_real,
         rho_imag,
         hamiltonian,
@@ -305,6 +721,20 @@
         table,
     )
 
+    def plain(*given):
+        return run_plain(peers, cap, mat_dev, link_count, sites, given[:8])
+
+    if peers % 32 or max(2, 2 * links // peers) != 2 * DIRECT or links != 128:
+        return plain(*arrays)
+    all_tables, worst = run_tables(peers, mat_dev, table)
+    return lax.cond(
+        worst[0, 0] <= PACKED,
+        lambda *given: run_packed(peers, mat_dev, link_count, sites, given),
+        plain,
+        *arrays,
+        all_tables,
+    )
+
 
 def solution(mesh):
     split_3 = P("aux", None, None)

time: 120 us -> 110 us (0.917)
  Pallas kernels: 114 us -> 102 us
    pallas_call x1 -> x2, Pallas kernels: 114 us -> 102 us  [the longest x1 90.9 us: run_packed(): pl.pallas_call(functools.partial(packed_kernel, peers, mat_dev, link_coun...]
    unnamed x10 -> x16, local copies, waits for them, and re-layouts: 4.59 us -> 4.14 us
where the time goes in v1:
time: 110 us; the launch traced here: 109 us
  Pallas kernels  102 us (93%)
  local copies, waits for them, and re-layouts  5.56 us (5%)
  between operations  1.36 us (1%)
    pallas_call x1, Pallas kernels, run_packed(): pl.pallas_call(functools.partial(packed_kernel, peers, mat_dev, link_coun...  90.9 us
    pallas_call x1, Pallas kernels, run_tables(): pl.pallas_call(functools.partial(read_tables, peers, mat_dev), out_shape=...  11.5 us
    unnamed x16, local copies, waits for them, and re-layouts  4.14 us

profile of v1, /device:TPU:0, one launch (start us, length us, event | category | flops | bytes accessed | tf_op | source)
XLA Modules:
  0.0 109.3 jit_solution(15277168498623280423)
XLA Ops:
  0.6 0.0 copy-start.4
  0.6 0.7 copy-done.4
  1.3 0.0 copy-start.5
  1.3 0.1 stack.12
  1.4 0.6 copy-done.5
  2.0 0.0 copy-start.6
  2.0 0.1 stack.13
  2.1 0.6 copy-done.6
  2.7 0.1 stack.14
  2.8 11.5 %shard_map.117 = (s32[2,32,128]{2,1,0:T(8,128)S(1)}, s32[8,128]{1,0:T(8,128)}) custom-call(s32[3,128]{1,0:T(4,128)S(1)} %pad_add_fusion.table), custom_call_target="tpu_custom_call" | custom-call | tf_op jit(solution)/shard_map/pallas_call | solution.py:677
  14.3 1.2 %slice.3 = s32[1,1]{1,0:T(1,128)} slice(s32[8,128]{1,0:T(8,128)} %get-tuple-element.55), slice={[0:1], [0:1]} | slice | bytes 8 | tf_op jit(solution)/shard_map/slice | solution.py:731
  15.5 0.0 copy-start.3
  16.1 0.0 copy-start.1
  16.1 0.0 copy-start.2
  16.2 0.0 copy-start
  16.2 0.0 copy-done.3
  16.2 0.6 copy-done.1
  16.8 0.0 copy-done.2
  16.8 0.0 copy-done
  16.9 90.9 %conditional.1 = ((f32[2,256,256]{2,1,0:T(8,128)S(1)}, f32[2,256,256]{2,1,0:T(8,128)S(1)})) conditional(s32[]{:T(128)} %bitcast, (f32[2,256,256]{2,1,0:T(8,128)}, f32[2,256,256]{2,1,0:T(8,128)}, f32[256,256]{1,0:T(8,128)}, f32[1,256]{1,0:T(1,128)S(1)}, f32[1,256]{1,0:T(1,128)S(1)}, /*index=5*/f32[1,256]{1,0:T(1,128)S(1)}, f32[1,256]{1,0:T(1,128)S(1)}, ...), branch_computations={%region_0.0_spmd, %region_1.0_spmd} | conditional | bytes 8 | solution.py:730
  16.9 90.9 %branch_1_fun.1 = (f32[2,256,256]{2,1,0:T(8,128)S(1)}, f32[2,256,256]{2,1,0:T(8,128)S(1)}) custom-call(f32[2,256,256]{2,1,0:T(8,128)} %get-tuple-element.42.rho_re, f32[2,256,256]{2,1,0:T(8,128)} %get-tuple-element.43.rho_im, f32[256,256]{1,0:T(8,128)} %get-tuple-element.44.ham_in, f32[1,256]{1,0:T(1,128)S(1)} %get-tuple-element.45.damping, ...), custom_call_target="tpu_custom_call" | custom-call | tf_op jit(solution)/shard_map/cond/branch_1_fun/pallas_call | solution.py:639
  107.7 0.8 copy.22
  108.5 0.8 copy.23
  (1 shorter events, 0.0 us)
Async XLA Ops:
  0.6 0.7 copy-start.4
  1.3 0.7 copy-start.5
  2.0 0.7 copy-start.6
  15.5 0.7 copy-start.3
  16.1 0.7 copy-start.1
  16.1 0.7 copy-start.2
  16.2 0.7 copy-start

commit v2 on v1

--- a/solution.py
+++ b/solution.py
@@ -361,8 +361,9 @@
     ham,
     acc,
     base,
-    ask_high,
+    ask_part,
     spread_all,
+    gammas,
     pick,
     spread,
     put,
@@ -441,72 +442,83 @@
         return lax.broadcasted_iota(jnp.int32, (block, 128), 1) == target
 
     mine = asked_of(me)
-    asked_mirror = asked_of(mirror)
-    high_all = ask_matrix(as_rows(mine, DIRECT))
-    ask_high[...] = high_all.astype(F32)
+    side = half * 8
+    far = slice(0, side)
+    packed = slice(side, side + 2 * PACKED)
+    close = slice(side + 2 * PACKED, 2 * side + 2 * PACKED)
+    extra = slice(2 * side + 2 * PACKED, 3 * side + 2 * PACKED)
+    ask_low = ask_matrix(as_rows(mine, 0))
+    ask_part[...] = ask_low.astype(F32)
+    home_rows = pl.ds(pl.multiple_of(home * 8, 128), side)
+    pick[far, 0 : 2 * depth] = ask_part[pl.ds(pl.multiple_of(away * 8, 128), side), :].astype(BF16)
+    pick[close, 0 : 2 * depth] = ask_part[home_rows, :].astype(BF16)
+    ask_high = ask_matrix(as_rows(mine, DIRECT))
+    ask_part[...] = ask_high.astype(F32)
     pack = jnp.where(packing(mine, 1 - me // half), 1.0, 0.0).T[0 : 2 * PACKED, :].astype(BF16)
-    spread_all[...] = jnp.where(packing(asked_mirror, me // half), 1.0, 0.0)
-    pick[0:block, 0 : 2 * depth] = ask_matrix(as_rows(mine, 0))
-    pick[block : block + half * 8, 0 : 2 * depth] = ask_high[
-        pl.ds(pl.multiple_of(home * 8, 128), half * 8), :
-    ].astype(BF16)
-    pick[block + half * 8 :, 0 : 2 * depth] = dot(pack, high_all).astype(BF16)
+    pick[packed, 0 : 2 * depth] = dot(pack, ask_high).astype(BF16)
+    pick[extra, 0 : 2 * depth] = ask_part[home_rows, :].astype(BF16)
     pick[:, 2 * depth :] = pick[:, 0 : 2 * depth]
-    spread[...] = spread_all[pl.ds(pl.multiple_of(home * 8, 128), half * 8), :].astype(BF16)
-
-    neighbor = table[0:1, :]
-    owner = neighbor // mat_dev
-    owner_here = jnp.broadcast_to(owner.astype(F32), (links, links))
-    same = jnp.where((owner_here == owner_here.T) & (first < second), 1.0, 0.0)
-    rank = jnp.sum(same, axis=0, keepdims=True).astype(jnp.int32)
-    landing = (rank // DIRECT) * block + owner * 8 + rank % DIRECT
-    lane = lax.broadcasted_iota(jnp.int32, (1, links), 1)
-    holder = lane // link_count
-    upward = (lane - holder * link_count < link_count - DOWN).astype(jnp.int32)
-    code = table[1:2, :] + sites * (holder + mat_dev * (upward + 2 * table[2:3, :]))
-    slot_index = lax.broadcasted_iota(jnp.int32, (slots, links), 0)
-    slot_base = slot_index - DIRECT * ((slot_index // DIRECT) % 2)
-    code_slot = (
-        jnp.sum(
-            jnp.where(slot_base == landing, (code + 1).astype(F32), 0.0), axis=1, keepdims=True
-        ).astype(jnp.int32)
-        - 1
-    )
-    used = code_slot >= 0
-    safe = jnp.maximum(code_slot, 0)
-    site_slot = jnp.where(used, safe % sites, -1)
-    rest = safe // sites
-    holder_slot = jnp.where(used, rest % mat_dev, -1)
-    rest = rest // mat_dev
-    up_slot = used & (rest % 2 == 1)
-    occ_slot = jnp.where(used, (rest // 2).astype(F32), 0.0)
-    own_site = lax.broadcasted_iota(jnp.int32, (slots, sites), 1) == site_slot
-
-    def look_up(ref):
-        return jnp.sum(jnp.where(own_site, ref[...], 0.0), axis=1, keepdims=True)
-
-    component = (lax.broadcasted_iota(jnp.int32, (slots, 1), 0) // DIRECT) % 2
-    part_re = jnp.where(up_slot, 0.0, occ_slot * look_up(bath_im))
-    part_im = jnp.where(up_slot, look_up(up_scale) * jnp.sqrt(occ_slot), occ_slot * look_up(bath_re))
-    part_im = jnp.where(component == 0, part_im, -part_im)
-    coef_re[...] = jnp.broadcast_to(part_re, (slots, sites))
-    coef_im[...] = jnp.broadcast_to(part_im, (slots, sites))
-    rate = jnp.where(up_slot | (component == 1), 0.0, occ_slot * look_up(damping))
-    gamma = [
-        jnp.sum(jnp.where(holder_slot == m, rate, 0.0), axis=0, keepdims=True)
-        for m in range(mat_dev)
-    ]
-    target = jnp.where(used, component * depth + holder_slot * sites + site_slot, -1)
-    target = jnp.broadcast_to(target.astype(F32), (slots, 128)).T[0:1, :].astype(jnp.int32)
-    placed = lax.broadcasted_iota(jnp.int32, (2 * depth, slots), 0) == target
-    placed = jnp.where(placed, 1.0, 0.0).astype(BF16)
-    put[:, 0:slots] = placed
-    put[:, slots:] = placed
-
-    ham[...] = 0.5 * (ham_in[...] + ham_in[...].T)
+
+    def settle():
+        asked_mirror = asked_of(mirror)
+        spread_all[...] = jnp.where(packing(asked_mirror, me // half), 1.0, 0.0)
+        spread[...] = spread_all[home_rows, :].astype(BF16)
+        ham[...] = 0.5 * (ham_in[...] + ham_in[...].T)
+        acc[...] = jnp.zeros_like(acc)
+
+        neighbor = table[0:1, :]
+        owner = neighbor // mat_dev
+        owner_here = jnp.broadcast_to(owner.astype(F32), (links, links))
+        same = jnp.where((owner_here == owner_here.T) & (first < second), 1.0, 0.0)
+        rank = jnp.sum(same, axis=0, keepdims=True).astype(jnp.int32)
+        landing = (rank // DIRECT) * block + owner * 8 + rank % DIRECT
+        lane = lax.broadcasted_iota(jnp.int32, (1, links), 1)
+        holder = lane // link_count
+        upward = (lane - holder * link_count < link_count - DOWN).astype(jnp.int32)
+        code = table[1:2, :] + sites * (holder + mat_dev * (upward + 2 * table[2:3, :]))
+        slot_index = lax.broadcasted_iota(jnp.int32, (slots, links), 0)
+        slot_base = slot_index - DIRECT * ((slot_index // DIRECT) % 2)
+        code_slot = (
+            jnp.sum(
+                jnp.where(slot_base == landing, (code + 1).astype(F32), 0.0), axis=1, keepdims=True
+            ).astype(jnp.int32)
+            - 1
+        )
+        used = code_slot >= 0
+        safe = jnp.maximum(code_slot, 0)
+        site_slot = jnp.where(used, safe % sites, -1)
+        rest = safe // sites
+        holder_slot = jnp.where(used, rest % mat_dev, -1)
+        rest = rest // mat_dev
+        up_slot = used & (rest % 2 == 1)
+        occ_slot = jnp.where(used, (rest // 2).astype(F32), 0.0)
+        own_site = lax.broadcasted_iota(jnp.int32, (slots, sites), 1) == site_slot
+
+        def look_up(ref):
+            return jnp.sum(jnp.where(own_site, ref[...], 0.0), axis=1, keepdims=True)
+
+        component = (lax.broadcasted_iota(jnp.int32, (slots, 1), 0) // DIRECT) % 2
+        part_re = jnp.where(up_slot, 0.0, occ_slot * look_up(bath_im))
+        part_im = jnp.where(up_slot, look_up(up_scale) * jnp.sqrt(occ_slot), occ_slot * look_up(bath_re))
+        part_im = jnp.where(component == 0, part_im, -part_im)
+        coef_re[...] = jnp.broadcast_to(part_re, (slots, sites))
+        coef_im[...] = jnp.broadcast_to(part_im, (slots, sites))
+        rate = jnp.where(up_slot | (component == 1), 0.0, occ_slot * look_up(damping))
+        gamma = [
+            jnp.sum(jnp.where(holder_slot == m, rate, 0.0), axis=0, keepdims=True)
+            for m in range(mat_dev)
+        ]
+        target = jnp.where(used, component * depth + holder_slot * sites + site_slot, -1)
+        target = jnp.broadcast_to(target.astype(F32), (slots, 128)).T[0:1, :].astype(jnp.int32)
+        placed = lax.broadcasted_iota(jnp.int32, (2 * depth, slots), 0) == target
+        placed = jnp.where(placed, 1.0, 0.0).astype(BF16)
+        put[:, 0:slots] = placed
+        put[:, slots:] = placed
+        for m in range(mat_dev):
+            gammas[m] = jnp.broadcast_to(gamma[m], (8, 128))
+
     cur_re[...] = rho_re[...]
     cur_im[...] = rho_im[...]
-    acc[...] = jnp.zeros_like(acc)
     pl.semaphore_wait(barrier, peers - 1)
 
     def send(source, target, t, kind, peer):
@@ -528,10 +540,11 @@
                 stack[2 * depth + at : 2 * depth + at + sites, :] = low
                 wide[:, at : at + sites] = high
                 wide[:, 2 * depth + at : 2 * depth + at + sites] = low
-        for p, pieces in enumerate((dot(pick[...], stack[...]), dot(pick[...], wide[...], NT))):
-            send_low[t, :, p] = pieces[0:block].reshape(peers, 8, sites)
-            send_high[t, :, p] = pieces[block : block + half * 8].reshape(half, 8, sites)
-            send_pack[t, p] = pieces[block + half * 8 :]
+        for p in range(2):
+            rows = slice(0, side + 2 * PACKED)
+            pieces = dot(pick[rows], wide[...], NT) if p else dot(pick[rows], stack[...])
+            send_low[t, pl.ds(away, half), p] = pieces[0:side].reshape(half, 8, sites)
+            send_pack[t, p] = pieces[side:]
 
         send(send_pack.at[t], recv_pack.at[t], t, 2, mirror).start()
 
@@ -548,9 +561,15 @@
             return c
 
         lax.fori_loop(0, half, across, 0)
+        for p in range(2):
+            rows = slice(side + 2 * PACKED, 3 * side + 2 * PACKED)
+            pieces = dot(pick[rows], wide[...], NT) if p else dot(pick[rows], stack[...])
+            send_low[t, pl.ds(home, half), p] = pieces[0:side].reshape(half, 8, sites)
+            send_high[t, :, p] = pieces[side:].reshape(half, 8, sites)
         lax.fori_loop(1, half, near, 0)
         recv_low[t, me] = send_low[t, me]
         recv_high[t, me] = send_high[t, place]
+        pl.when(t == 0)(settle)
 
         last = t == 3
         weight = jnp.where(last, STEP_SIZE / 6.0, jnp.where(t == 2, STEP_SIZE, 0.5 * STEP_SIZE))
@@ -566,8 +585,9 @@
             comm_im = exact_dot(ham[...], here_im) - exact_dot(here_im, ham[...])
             from_re = jnp.where(last, acc_re, rho_re[m])
             from_im = jnp.where(last, acc_im, rho_im[m])
-            base[m, 0] = from_re + weight * (comm_im - gamma[m] * here_re)
-            base[m, 1] = from_im - weight * (comm_re + gamma[m] * here_im)
+            gamma = gammas[m][0:1, 0:1]
+            base[m, 0] = from_re + weight * (comm_im - gamma * here_re)
+            base[m, 1] = from_im - weight * (comm_re + gamma * here_im)
 
         for m in range(mat_dev // 2):
             alone(m)
@@ -654,6 +674,7 @@
             pltpu.VMEM((mat_dev, 2, sites, sites), F32),
             pltpu.VMEM((peers * 8, 2 * depth), F32),
             pltpu.VMEM((peers * 8, 128), F32),
+            pltpu.VMEM((mat_dev, 8, 128), F32),
             pltpu.VMEM((rows, 4 * depth), BF16),
             pltpu.VMEM((half * 8, 128), BF16),
             pltpu.VMEM((2 * depth, 2 * slots), BF16),

time: 110 us -> 108 us (0.982)
    pallas_call x1, Pallas kernels: 90.9 us -> 89.6 us  [run_packed(): pl.pallas_call(functools.partial(packed_kernel, peers, mat_dev, link_coun...]
where the time goes in v2:
time: 108 us
  Pallas kernels  101 us (94%)
  local copies, waits for them, and re-layouts  5.56 us (5%)
  between operations  1.36 us (1%)
    pallas_call x1, Pallas kernels, run_packed(): pl.pallas_call(functools.partial(packed_kernel, peers, mat_dev, link_coun...  89.6 us
    pallas_call x1, Pallas kernels, run_tables(): pl.pallas_call(functools.partial(read_tables, peers, mat_dev), out_shape=...  11.5 us
    unnamed x16, local copies, waits for them, and re-layouts  4.14 us

profile of v2, /device:TPU:0, one launch (start us, length us, event | category | flops | bytes accessed | tf_op | source)
XLA Modules:
  0.0 108.0 jit_solution(4130969179468040120)
XLA Ops:
  0.6 0.0 copy-start.4
  0.6 0.7 copy-done.4
  1.3 0.0 copy-start.5
  1.3 0.1 stack.12
  1.4 0.6 copy-done.5
  2.0 0.0 copy-start.6
  2.0 0.1 stack.13
  2.1 0.6 copy-done.6
  2.7 0.1 stack.14
  2.8 11.5 %shard_map.117 = (s32[2,32,128]{2,1,0:T(8,128)S(1)}, s32[8,128]{1,0:T(8,128)}) custom-call(s32[3,128]{1,0:T(4,128)S(1)} %pad_add_fusion.table), custom_call_target="tpu_custom_call" | custom-call | tf_op jit(solution)/shard_map/pallas_call | solution.py:698
  14.3 1.2 %slice.3 = s32[1,1]{1,0:T(1,128)} slice(s32[8,128]{1,0:T(8,128)} %get-tuple-element.55), slice={[0:1], [0:1]} | slice | bytes 8 | tf_op jit(solution)/shard_map/slice | solution.py:752
  15.5 0.0 copy-start.3
  16.1 0.0 copy-start.1
  16.1 0.0 copy-start.2
  16.2 0.0 copy-start
  16.2 0.0 copy-done.3
  16.2 0.6 copy-done.1
  16.8 0.0 copy-done.2
  16.8 0.0 copy-done
  16.9 89.6 %conditional.1 = ((f32[2,256,256]{2,1,0:T(8,128)S(1)}, f32[2,256,256]{2,1,0:T(8,128)S(1)})) conditional(s32[]{:T(128)} %bitcast, (f32[2,256,256]{2,1,0:T(8,128)}, f32[2,256,256]{2,1,0:T(8,128)}, f32[256,256]{1,0:T(8,128)}, f32[1,256]{1,0:T(1,128)S(1)}, f32[1,256]{1,0:T(1,128)S(1)}, /*index=5*/f32[1,256]{1,0:T(1,128)S(1)}, f32[1,256]{1,0:T(1,128)S(1)}, ...), branch_computations={%region_0.0_spmd, %region_1.0_spmd} | conditional | bytes 8 | solution.py:751
  16.9 89.6 %branch_1_fun.1 = (f32[2,256,256]{2,1,0:T(8,128)S(1)}, f32[2,256,256]{2,1,0:T(8,128)S(1)}) custom-call(f32[2,256,256]{2,1,0:T(8,128)} %get-tuple-element.42.rho_re, f32[2,256,256]{2,1,0:T(8,128)} %get-tuple-element.43.rho_im, f32[256,256]{1,0:T(8,128)} %get-tuple-element.44.ham_in, f32[1,256]{1,0:T(1,128)S(1)} %get-tuple-element.45.damping, ...), custom_call_target="tpu_custom_call" | custom-call | tf_op jit(solution)/shard_map/cond/branch_1_fun/pallas_call | solution.py:659
  106.5 0.8 copy.22
  107.3 0.8 copy.23
  (1 shorter events, 0.0 us)
Async XLA Ops:
  0.6 0.7 copy-start.4
  1.3 0.7 copy-start.5
  2.0 0.7 copy-start.6
  15.5 0.7 copy-start.3
  16.1 0.7 copy-start.1
  16.1 0.7 copy-start.2
  16.2 0.7 copy-start
